TPU v7x, 32 devices: a whole 2x2x4 slice. The times are simulated.
32 devices in a mesh: layer: 8 (over z, x), batch: 4 (over y, core).
Axes of the slice: x: 2, y: 2, z: 4, core: 2. Of those that a mesh axis runs over, the one named last changes fastest.
Arguments:
- first_state: float32 [4, 32, 32, 256], P('batch'), may hold values from -6 to 6
- guess_points: float32 [8, 4, 32, 32, 256], P('layer', 'batch'), may hold values from -6 to 6
- weights: bfloat16 [32, 3, 3, 256, 256], P('layer'), may hold values from -0.5 to 0.5
Outputs:
- states: float32 [32, 4, 32, 32, 256], P('layer', 'batch')
- norms: float32 [8], P('layer')
All inputs are finite; a program needn't handle non-finite values.
Results may differ from a plain program's by a relative error of at most 0.0038.
Values sent between devices are 32-bit elements; how exact they have to be, the bound alone decides.
A program may use at most 128 MiB of HBM per device.

v0:
```python
import functools

import jax
import jax.numpy as jnp
from jax import lax
from jax.experimental import pallas as pl
from jax.experimental.pallas import tpu as pltpu
from jax.sharding import PartitionSpec as P

BLOCK = 4


def passed_along(block, axis, distance):
    devices = range(lax.axis_size(axis))
    route = [(i - distance, i) for i in devices if i - distance in devices]
    return lax.ppermute(block, axis, route)


def propagate(state, weight, factor):
    mixed = lax.conv_general_dilated(
        state.astype(jnp.bfloat16),
        weight,
        (1, 1),
        "SAME",
        dimension_numbers=("NHWC", "HWIO", "NHWC"),
        preferred_element_type=jnp.float32,
    )
    return state + factor * jax.nn.relu(mixed)


def per_device(first_state, guess_points, weights):
    blocks_here = lax.axis_size("layer")
    step_size = 2.0 / (BLOCK * blocks_here)
    layer_index = lax.axis_index("layer")
    position = layer_index % 4
    is_first = layer_index == 0
    zeros_state = jnp.zeros_like(first_state)

    def block_sweep(state):
        for slot in range(BLOCK):
            state = propagate(state, weights[slot], step_size)
        return state

    from_left = passed_along(guess_points[0], "layer", 1)
    relaxed = block_sweep(jnp.where(is_first, first_state, from_left))
    from_left = passed_along(relaxed, "layer", 1)
    entry_state = jnp.where(is_first, first_state, from_left)
    swept = block_sweep(entry_state)
    residual = swept - relaxed
    square_sum = lax.psum(jnp.sum(residual * residual), "batch")
    entries = residual.size * lax.axis_size("batch")
    norms = jnp.reshape(jnp.sqrt(square_sum / entries + 1e-06), (1,))
    coarse_weight = weights[0]
    fine_rhs = swept - propagate(entry_state, coarse_weight, 4.0 * step_size)

    def coarse_apply(state):
        return propagate(state, coarse_weight, 4.0 * step_size) + fine_rhs

    def coarse_chain(carry_out, length):
        moving = zeros_state
        taken = zeros_state
        for turn_index in range(length):
            outgoing = jnp.where(position == 3, carry_out, moving)
            received = passed_along(outgoing, "layer", 1)
            incoming = jnp.where(is_first, first_state, received)
            moving = lax.cond(
                position == turn_index,
                lambda fresh, kept: coarse_apply(fresh),
                lambda fresh, kept: kept,
                incoming,
                moving,
            )
            taken = jnp.where(position == turn_index, incoming, taken)
        return (moving, taken)

    group_ends, unused_taken = coarse_chain(relaxed, BLOCK)
    swept_ends, previous_ends = coarse_chain(group_ends, BLOCK)
    predicted = lax.cond(
        position == 0,
        lambda state: propagate(state, coarse_weight, 16.0 * step_size),
        lambda state: jnp.zeros_like(state),
        previous_ends,
    )

    def coarse_delta(received_state):
        earlier = jnp.where(is_first, first_state, received_state)
        return (earlier, propagate(earlier, coarse_weight, 16.0 * step_size) - predicted)

    def branch_of(turn_index):
        kind = jnp.where(position == 0, 0, jnp.where(position == 3, 2, 1))
        return jnp.where(layer_index == turn_index, kind, 3)

    def relay_single(turn_index, carried):
        sending, own_value = carried
        got = passed_along(sending, "layer", 1)

        def head_step(got_in, sent, kept):
            earlier, delta = coarse_delta(got_in)
            return (delta, kept)

        def middle_step(got_in, sent, kept):
            return (got_in, kept)

        def tail_step(got_in, sent, kept):
            value = got_in + swept_ends
            return (value, value)

        def keep_step(got_in, sent, kept):
            return (sent, kept)

        return lax.switch(
            branch_of(turn_index),
            [head_step, middle_step, tail_step, keep_step],
            got,
            sending,
            own_value,
        )

    sending, coarse_own = lax.fori_loop(0, blocks_here, relay_single, (zeros_state, zeros_state))
    corrected, unused_entry = coarse_chain(coarse_own, BLOCK - 1)
    coarse_final = jnp.where(position == 3, coarse_own, corrected)
    from_left = passed_along(coarse_final, "layer", 1)
    moving = jnp.where(is_first, first_state, from_left)
    results = []
    for slot in range(BLOCK - 1):
        moving = propagate(moving, weights[slot], step_size)
        results.append(moving)
    results.append(coarse_final)
    return (jnp.stack(results), norms)


PASS_ROWS = 8
CHAIN_ROWS = 4


def cycle_kernel(
    layers_axis,
    batch_axis,
    first_ref,
    guess_ref,
    weights_ref,
    out_ref,
    norm_ref,
    guess_in,
    entry_in,
    coarse_in,
    work,
    relaxed_ref,
    rhs_ref,
    taps_a,
    taps_b,
    partial_ref,
    guess_send,
    guess_recv,
    entry_send,
    entry_recv,
    coarse_send,
    coarse_recv,
    norm_send,
    norm_recv,
):
    rows, width, channels = first_ref.shape
    step_size = 2.0 / (BLOCK * layers_axis)
    me = lax.axis_index("layer")
    my_batch = lax.axis_index("batch")
    last = layers_axis - 1
    passes = rows // PASS_ROWS
    pieces = rows // CHAIN_ROWS

    def strip(index, count):
        return pl.ds(pl.multiple_of(index * count, count), count)

    def to_right(source, target, send, recv):
        return pltpu.make_async_remote_copy(
            src_ref=source,
            dst_ref=target,
            send_sem=send,
            recv_sem=recv,
            device_id={"layer": me + 1},
            device_id_type=pl.DeviceIdType.MESH,
        )

    def guess_copy(index):
        at = strip(index, PASS_ROWS)
        return to_right(guess_ref.at[at], guess_in.at[at], guess_send.at[index], guess_recv.at[index])

    def entry_copy(index):
        at = strip(index, PASS_ROWS)
        return to_right(relaxed_ref.at[at], entry_in.at[at], entry_send.at[index], entry_recv.at[index])

    def coarse_copy(index):
        at = strip(index, CHAIN_ROWS)
        return to_right(out_ref.at[3, at], coarse_in.at[at], coarse_send.at[index], coarse_recv.at[index])

    def norm_copy(offset):
        return pltpu.make_async_remote_copy(
            src_ref=partial_ref.at[my_batch],
            dst_ref=partial_ref.at[my_batch],
            send_sem=norm_send.at[offset],
            recv_sem=norm_recv.at[offset],
            device_id={"batch": lax.rem(my_batch + offset, batch_axis)},
            device_id_type=pl.DeviceIdType.MESH,
        )

    barrier = pltpu.get_barrier_semaphore()

    @pl.when(me > 0)
    def _():
        pl.semaphore_signal(barrier, inc=1, device_id={"layer": me - 1}, device_id_type=pl.DeviceIdType.MESH)

    @pl.when(me < last)
    def _():
        pl.semaphore_signal(barrier, inc=1, device_id={"layer": me + 1}, device_id_type=pl.DeviceIdType.MESH)

    for offset in range(1, batch_axis):
        pl.semaphore_signal(
            barrier,
            inc=1,
            device_id={"batch": lax.rem(my_batch + offset, batch_axis)},
            device_id_type=pl.DeviceIdType.MESH,
        )
    others = batch_axis - 1 + jnp.where(me > 0, 1, 0) + jnp.where(me < last, 1, 0)
    pl.semaphore_wait(barrier, others)

    @pl.when(me < last)
    def _():
        for index in range(passes):
            guess_copy(index).start()

    @pl.when(me == 0)
    def _():
        guess_in[...] = first_ref[...]
        entry_in[...] = first_ref[...]

    for taps in (taps_a, taps_b):
        edge = jnp.zeros((width, 3 * channels), taps.dtype)
        taps[pl.ds(0, width), :] = edge
        taps[pl.ds((rows + 1) * width, width), :] = edge

    def put_taps(taps, index, count, block):
        flat = block.reshape(count * width, channels)
        column = lax.rem(lax.broadcasted_iota(jnp.int32, flat.shape, 0), width)
        before = jnp.where(column == 0, 0.0, pltpu.roll(flat, 1, 0))
        after = jnp.where(column == width - 1, 0.0, pltpu.roll(flat, count * width - 1, 0))
        at = pl.ds(pl.multiple_of((index * count + 1) * width, width), count * width)
        taps[at, pl.ds(0, channels)] = before.astype(taps.dtype)
        taps[at, pl.ds(channels, channels)] = flat.astype(taps.dtype)
        taps[at, pl.ds(2 * channels, channels)] = after.astype(taps.dtype)

    def mixed(taps, slot, index, count):
        total = None
        for down in range(3):
            at = pl.ds(pl.multiple_of((index * count + down) * width, width), count * width)
            part = jnp.dot(taps[at, :], weights_ref[slot, down], preferred_element_type=jnp.float32)
            total = part if total is None else total + part
        return jnp.maximum(total, 0.0).reshape(count, width, channels)

    def one_pass(taps, slot, count, emit, carry=0, arrive=None):
        if arrive is not None:
            arrive(0)

        def body(index, carry):
            if arrive is not None:

                @pl.when(index + 1 < rows // count)
                def _():
                    arrive(index + 1)

            return emit(index, strip(index, count), mixed(taps, slot, index, count), carry)

        return lax.fori_loop(0, rows // count, body, carry)

    def guess_arrives(index):
        @pl.when(me > 0)
        def _():
            guess_copy(index).wait_recv()

        put_taps(taps_a, index, PASS_ROWS, guess_in[strip(index, PASS_ROWS)])

    def relax_step(source, target, taps_next):
        def emit(index, at, active, carry):
            block = source[at] + step_size * active
            target[at] = block
            if taps_next is not None:
                put_taps(taps_next, index, PASS_ROWS, block)
            else:

                @pl.when(me < last)
                def _():
                    entry_copy(index).start()

            return carry

        return emit

    one_pass(taps_a, 0, PASS_ROWS, relax_step(guess_in, work, taps_b), arrive=guess_arrives)
    one_pass(taps_b, 1, PASS_ROWS, relax_step(work, work, taps_a))
    one_pass(taps_a, 2, PASS_ROWS, relax_step(work, work, taps_b))
    one_pass(taps_b, 3, PASS_ROWS, relax_step(work, relaxed_ref, None))

    def entry_arrives(index):
        @pl.when(me > 0)
        def _():
            entry_copy(index).wait_recv()

        put_taps(taps_a, index, PASS_ROWS, entry_in[strip(index, PASS_ROWS)])

    def sweep_first(index, at, active, carry):
        block = entry_in[at]
        rhs_ref[at] = block + 4.0 * step_size * active
        block = block + step_size * active
        out_ref[0, at] = block
        put_taps(taps_b, index, PASS_ROWS, block)
        return carry

    def sweep_middle(slot, taps_next):
        def emit(index, at, active, carry):
            block = out_ref[slot - 1, at] + step_size * active
            out_ref[slot, at] = block
            put_taps(taps_next, index, PASS_ROWS, block)
            return carry

        return emit

    def sweep_last(index, at, active, squares):
        block = out_ref[2, at] + step_size * active
        out_ref[3, at] = block
        rhs_ref[at] = block - rhs_ref[at]

        @pl.when(jnp.logical_and(me == 1, me < last))
        def _():
            for piece in range(PASS_ROWS // CHAIN_ROWS):
                coarse_copy(index * (PASS_ROWS // CHAIN_ROWS) + piece).start()

        gap = (block - relaxed_ref[at]).reshape(-1, 8, channels)
        return squares + jnp.sum(gap * gap, axis=0)

    one_pass(taps_a, 0, PASS_ROWS, sweep_first, arrive=entry_arrives)
    one_pass(taps_b, 1, PASS_ROWS, sweep_middle(1, taps_a))
    one_pass(taps_a, 2, PASS_ROWS, sweep_middle(2, taps_b))
    squares = one_pass(taps_b, 3, PASS_ROWS, sweep_last, jnp.zeros((8, channels), jnp.float32))
    partial_ref[my_batch] = squares
    for offset in range(1, batch_axis):
        norm_copy(offset).start()

    def coarse_arrives(index):
        coarse_copy(index).wait_recv()
        put_taps(taps_a, index, CHAIN_ROWS, coarse_in[strip(index, CHAIN_ROWS)])

    def chain_emit(index, at, active, carry):
        block = coarse_in[at]
        out_ref[3, at] = block + 4.0 * step_size * active + rhs_ref[at]

        @pl.when(me < last)
        def _():
            coarse_copy(index).start()

        block = block + step_size * active
        out_ref[0, at] = block
        put_taps(taps_b, index, CHAIN_ROWS, block)
        return carry

    def final_emit(index, at, active, carry):
        out_ref[2, at] = out_ref[1, at] + step_size * active
        return carry

    @pl.when(me >= 2)
    def _():
        one_pass(taps_a, 0, CHAIN_ROWS, chain_emit, arrive=coarse_arrives)
        one_pass(taps_b, 1, PASS_ROWS, sweep_middle(1, taps_a))
        one_pass(taps_a, 2, PASS_ROWS, final_emit)

    for offset in range(1, batch_axis):
        norm_copy(offset).wait()
    gathered = partial_ref[0]
    for index in range(1, batch_axis):
        gathered = gathered + partial_ref[index]
    entries = rows * width * channels * batch_axis
    norm_ref[...] = jnp.broadcast_to(jnp.sqrt(jnp.sum(gathered, keepdims=True) / entries + 1e-06), norm_ref.shape)

    @pl.when(me < last)
    def _():
        for index in range(passes):
            guess_copy(index).wait_send()
            entry_copy(index).wait_send()

    @pl.when(jnp.logical_and(me >= 1, me < last))
    def _():
        for index in range(pieces):
            coarse_copy(index).wait_send()


def per_device_streamed(first_state, guess_points, weights):
    layers_axis = lax.axis_size("layer")
    batch_axis = lax.axis_size("batch")
    _, rows, width, channels = first_state.shape
    state = (rows, width, channels)
    taps = ((rows + 2) * width, 3 * channels)
    passes, pieces = rows // PASS_ROWS, rows // CHAIN_ROWS
    in_vmem = pl.BlockSpec(memory_space=pltpu.VMEM)
    states, norms = pl.pallas_call(
        functools.partial(cycle_kernel, layers_axis, batch_axis),
        out_shape=(
            jax.ShapeDtypeStruct((BLOCK,) + state, jnp.float32),
            jax.ShapeDtypeStruct((8, 128), jnp.float32),
        ),
        in_specs=[in_vmem] * 3,
        out_specs=(in_vmem, in_vmem),
        scratch_shapes=[pltpu.VMEM(state, jnp.float32)] * 6
        + [pltpu.VMEM(taps, jnp.bfloat16)] * 2
        + [pltpu.VMEM((batch_axis, 8, channels), jnp.float32)]
        + [pltpu.SemaphoreType.DMA((passes,))] * 4
        + [pltpu.SemaphoreType.DMA((pieces,))] * 2
        + [pltpu.SemaphoreType.DMA((batch_axis,))] * 2,
        compiler_params=pltpu.CompilerParams(
            collective_id=0, has_side_effects=True, vmem_limit_bytes=48 * 1024 * 1024
        ),
    )(first_state[0], guess_points[0, 0], weights.reshape(BLOCK, 3, 3 * channels, channels))
    return (states[:, None], norms[0, :1])


def solution(mesh):
    placed = (
        P("batch", None, None, None),
        P("layer", "batch", None, None, None),
        P("layer", None, None, None, None),
    )
    return jax.shard_map(
        per_device if mesh.shape["layer"] // BLOCK > 2 else per_device_streamed,
        mesh=mesh,
        in_specs=placed,
        out_specs=(P("layer", "batch", None, None, None), P("layer")),
        check_vma=False,
    )
```

profile of v0, /device:TPU:26, one launch (start us, length us, event | category | flops | bytes accessed | tf_op | source)
XLA Modules:
  0.0 135.5 jit_solution(15213445745661426782)
XLA Ops:
  0.6 0.0 copy-start
  0.6 1.2 copy-done
  1.9 0.0 copy-start.1
  1.9 1.2 copy-done.1
  3.1 127.1 %shard_map.50 = (f32[4,32,32,256]{3,2,1,0:T(8,128)}, f32[8,128]{1,0:T(8,128)S(1)}) custom-call(f32[32,32,256]{2,1,0:T(8,128)S(1)} %bitcast.7, f32[32,32,256]{2,1,0:T(8,128)S(1)} %bitcast.8, bf16[4,3,768,256]{3,2,1,0:T(8,128)(2,1)} %bitcast.9), custom_call_target="tpu_custom_call" | custom-call | tf_op jit(solution)/shard_map/pallas_call | solution.py:401
  130.2 0.5 slice.3
  130.7 4.8 %copy.7 = f32[4,1,32,32,256]{4,3,2,1,0:T(8,128)} copy(f32[4,1,32,32,256]{4,3,2,1,0:T(8,128)} %bitcast.10) | data formatting | bytes 8388608
Async XLA Ops:
  0.6 1.2 copy-start
  1.9 1.2 copy-start.1
where the time goes:
time: 136 us
  Pallas kernels  127 us (93%)
  local copies, waits for them, and re-layouts  7.74 us (6%)
    pallas_call x1, Pallas kernels, per_device_streamed(): pl.pallas_call(functools.partial(cycle_kernel, layers_axis, batch_axis),...  127 us
    unnamed x5, local copies, waits for them, and re-layouts  7.23 us

commit v1 on v0

--- a/solution.py
+++ b/solution.py
@@ -129,8 +129,8 @@
     return (jnp.stack(results), norms)
 
 
-PASS_ROWS = 8
-CHAIN_ROWS = 4
+PASS_ROWS = 4
+CHAIN_ROWS = 2
 
 
 def cycle_kernel(
@@ -138,7 +138,7 @@
     batch_axis,
     first_ref,
     guess_ref,
-    weights_ref,
+    weights_hbm,
     out_ref,
     norm_ref,
     guess_in,
@@ -147,8 +147,13 @@
     work,
     relaxed_ref,
     rhs_ref,
-    taps_a,
-    taps_b,
+    taps_0,
+    taps_1,
+    taps_2,
+    taps_3,
+    squares_ref,
+    weights_ref,
+    load_sem,
     partial_ref,
     guess_send,
     guess_recv,
@@ -202,6 +207,8 @@
             device_id_type=pl.DeviceIdType.MESH,
         )
 
+    load_weights = pltpu.make_async_copy(weights_hbm, weights_ref, load_sem)
+    load_weights.start()
     barrier = pltpu.get_barrier_semaphore()
 
     @pl.when(me > 0)
@@ -229,10 +236,10 @@
 
     @pl.when(me == 0)
     def _():
-        guess_in[...] = first_ref[...]
-        entry_in[...] = first_ref[...]
-
-    for taps in (taps_a, taps_b):
+        pltpu.sync_copy(first_ref, guess_in)
+        entry_in[...] = guess_in[...]
+
+    for taps in (taps_0, taps_1, taps_2, taps_3):
         edge = jnp.zeros((width, 3 * channels), taps.dtype)
         taps[pl.ds(0, width), :] = edge
         taps[pl.ds((rows + 1) * width, width), :] = edge
@@ -255,74 +262,84 @@
             total = part if total is None else total + part
         return jnp.maximum(total, 0.0).reshape(count, width, channels)
 
-    def one_pass(taps, slot, count, emit, carry=0, arrive=None):
-        if arrive is not None:
-            arrive(0)
-
-        def body(index, carry):
-            if arrive is not None:
-
-                @pl.when(index + 1 < rows // count)
-                def _():
-                    arrive(index + 1)
-
-            return emit(index, strip(index, count), mixed(taps, slot, index, count), carry)
-
-        return lax.fori_loop(0, rows // count, body, carry)
+    def wave(count, arrive, steps):
+        chunks = rows // count
+
+        def body(turn, carry):
+            @pl.when(turn < chunks)
+            def _():
+                arrive(turn)
+
+            for behind, (taps, slot, emit) in enumerate(steps):
+                index = turn - 1 - behind
+
+                @pl.when(jnp.logical_and(index >= 0, index < chunks))
+                def _(index=index, taps=taps, slot=slot, emit=emit):
+                    emit(index, strip(index, count), mixed(taps, slot, index, count))
+
+            return carry
+
+        lax.fori_loop(0, chunks + len(steps), body, 0)
+
+    load_weights.wait()
 
     def guess_arrives(index):
         @pl.when(me > 0)
         def _():
             guess_copy(index).wait_recv()
 
-        put_taps(taps_a, index, PASS_ROWS, guess_in[strip(index, PASS_ROWS)])
-
-    def relax_step(source, target, taps_next):
-        def emit(index, at, active, carry):
+        put_taps(taps_0, index, PASS_ROWS, guess_in[strip(index, PASS_ROWS)])
+
+    def relax_step(source, taps_next):
+        def emit(index, at, active):
             block = source[at] + step_size * active
-            target[at] = block
-            if taps_next is not None:
-                put_taps(taps_next, index, PASS_ROWS, block)
-            else:
-
-                @pl.when(me < last)
-                def _():
-                    entry_copy(index).start()
-
-            return carry
+            work[at] = block
+            put_taps(taps_next, index, PASS_ROWS, block)
 
         return emit
 
-    one_pass(taps_a, 0, PASS_ROWS, relax_step(guess_in, work, taps_b), arrive=guess_arrives)
-    one_pass(taps_b, 1, PASS_ROWS, relax_step(work, work, taps_a))
-    one_pass(taps_a, 2, PASS_ROWS, relax_step(work, work, taps_b))
-    one_pass(taps_b, 3, PASS_ROWS, relax_step(work, relaxed_ref, None))
+    def relax_last(index, at, active):
+        relaxed_ref[at] = work[at] + step_size * active
+
+        @pl.when(me < last)
+        def _():
+            entry_copy(index).start()
+
+    wave(
+        PASS_ROWS,
+        guess_arrives,
+        (
+            (taps_0, 0, relax_step(guess_in, taps_1)),
+            (taps_1, 1, relax_step(work, taps_2)),
+            (taps_2, 2, relax_step(work, taps_3)),
+            (taps_3, 3, relax_last),
+        ),
+    )
 
     def entry_arrives(index):
         @pl.when(me > 0)
         def _():
             entry_copy(index).wait_recv()
 
-        put_taps(taps_a, index, PASS_ROWS, entry_in[strip(index, PASS_ROWS)])
-
-    def sweep_first(index, at, active, carry):
+        put_taps(taps_0, index, PASS_ROWS, entry_in[strip(index, PASS_ROWS)])
+
+    def sweep_first(index, at, active):
         block = entry_in[at]
         rhs_ref[at] = block + 4.0 * step_size * active
         block = block + step_size * active
         out_ref[0, at] = block
-        put_taps(taps_b, index, PASS_ROWS, block)
-        return carry
-
-    def sweep_middle(slot, taps_next):
-        def emit(index, at, active, carry):
+        put_taps(taps_1, index, PASS_ROWS, block)
+
+    def sweep_middle(slot, count, taps_next):
+        def emit(index, at, active):
             block = out_ref[slot - 1, at] + step_size * active
             out_ref[slot, at] = block
-            put_taps(taps_next, index, PASS_ROWS, block)
-            return carry
+            if taps_next is not None:
+                put_taps(taps_next, index, count, block)
 
         return emit
 
-    def sweep_last(index, at, active, squares):
+    def sweep_last(index, at, active):
         block = out_ref[2, at] + step_size * active
         out_ref[3, at] = block
         rhs_ref[at] = block - rhs_ref[at]
@@ -333,21 +350,28 @@
                 coarse_copy(index * (PASS_ROWS // CHAIN_ROWS) + piece).start()
 
         gap = (block - relaxed_ref[at]).reshape(-1, 8, channels)
-        return squares + jnp.sum(gap * gap, axis=0)
-
-    one_pass(taps_a, 0, PASS_ROWS, sweep_first, arrive=entry_arrives)
-    one_pass(taps_b, 1, PASS_ROWS, sweep_middle(1, taps_a))
-    one_pass(taps_a, 2, PASS_ROWS, sweep_middle(2, taps_b))
-    squares = one_pass(taps_b, 3, PASS_ROWS, sweep_last, jnp.zeros((8, channels), jnp.float32))
-    partial_ref[my_batch] = squares
+        squares_ref[...] += jnp.sum(gap * gap, axis=0)
+
+    squares_ref[...] = jnp.zeros_like(squares_ref)
+    wave(
+        PASS_ROWS,
+        entry_arrives,
+        (
+            (taps_0, 0, sweep_first),
+            (taps_1, 1, sweep_middle(1, PASS_ROWS, taps_2)),
+            (taps_2, 2, sweep_middle(2, PASS_ROWS, taps_3)),
+            (taps_3, 3, sweep_last),
+        ),
+    )
+    partial_ref[my_batch] = squares_ref[...]
     for offset in range(1, batch_axis):
         norm_copy(offset).start()
 
     def coarse_arrives(index):
         coarse_copy(index).wait_recv()
-        put_taps(taps_a, index, CHAIN_ROWS, coarse_in[strip(index, CHAIN_ROWS)])
-
-    def chain_emit(index, at, active, carry):
+        put_taps(taps_0, index, CHAIN_ROWS, coarse_in[strip(index, CHAIN_ROWS)])
+
+    def chain_step(index, at, active):
         block = coarse_in[at]
         out_ref[3, at] = block + 4.0 * step_size * active + rhs_ref[at]
 
@@ -357,18 +381,53 @@
 
         block = block + step_size * active
         out_ref[0, at] = block
-        put_taps(taps_b, index, CHAIN_ROWS, block)
-        return carry
-
-    def final_emit(index, at, active, carry):
-        out_ref[2, at] = out_ref[1, at] + step_size * active
-        return carry
+        put_taps(taps_1, index, CHAIN_ROWS, block)
+
+    def run(taps, slot, count, emit):
+        def body(index, carry):
+            emit(index, strip(index, count), mixed(taps, slot, index, count))
+            return carry
+
+        return body
+
+    chain_body = run(taps_0, 0, CHAIN_ROWS, chain_step)
+    second_body = run(taps_1, 1, CHAIN_ROWS, sweep_middle(1, CHAIN_ROWS, taps_2))
+    third_body = run(taps_2, 2, CHAIN_ROWS, sweep_middle(2, CHAIN_ROWS, None))
 
     @pl.when(me >= 2)
     def _():
-        one_pass(taps_a, 0, CHAIN_ROWS, chain_emit, arrive=coarse_arrives)
-        one_pass(taps_b, 1, PASS_ROWS, sweep_middle(1, taps_a))
-        one_pass(taps_a, 2, PASS_ROWS, final_emit)
+        def body(turn, carry):
+            coarse_arrives(turn)
+
+            @pl.when(turn >= 1)
+            def _():
+                chain_body(turn - 1, 0)
+
+            @pl.when(turn == pieces - 1)
+            def _():
+                chain_body(turn, 0)
+
+            @pl.when(jnp.logical_and(me == last, turn >= 2))
+            def _():
+                second_body(turn - 2, 0)
+
+            @pl.when(jnp.logical_and(me == last, turn >= 3))
+            def _():
+                third_body(turn - 3, 0)
+
+            return carry
+
+        lax.fori_loop(0, pieces, body, 0)
+
+        @pl.when(me == last)
+        def _():
+            lax.fori_loop(pieces - 2, pieces, second_body, 0)
+            lax.fori_loop(pieces - 3, pieces, third_body, 0)
+
+        @pl.when(me < last)
+        def _():
+            lax.fori_loop(0, passes, run(taps_1, 1, PASS_ROWS, sweep_middle(1, PASS_ROWS, taps_2)), 0)
+            lax.fori_loop(0, passes, run(taps_2, 2, PASS_ROWS, sweep_middle(2, PASS_ROWS, None)), 0)
 
     for offset in range(1, batch_axis):
         norm_copy(offset).wait()
@@ -401,21 +460,23 @@
     states, norms = pl.pallas_call(
         functools.partial(cycle_kernel, layers_axis, batch_axis),
         out_shape=(
-            jax.ShapeDtypeStruct((BLOCK,) + state, jnp.float32),
+            pltpu.VMEM((BLOCK,) + state, jnp.float32),
             jax.ShapeDtypeStruct((8, 128), jnp.float32),
         ),
-        in_specs=[in_vmem] * 3,
+        in_specs=[pl.BlockSpec(memory_space=pltpu.HBM)] * 3,
         out_specs=(in_vmem, in_vmem),
         scratch_shapes=[pltpu.VMEM(state, jnp.float32)] * 6
-        + [pltpu.VMEM(taps, jnp.bfloat16)] * 2
+        + [pltpu.VMEM(taps, jnp.bfloat16)] * 4
+        + [pltpu.VMEM((8, channels), jnp.float32)]
+        + [pltpu.VMEM((BLOCK, 3, 3 * channels, channels), jnp.bfloat16), pltpu.SemaphoreType.DMA]
         + [pltpu.VMEM((batch_axis, 8, channels), jnp.float32)]
         + [pltpu.SemaphoreType.DMA((passes,))] * 4
         + [pltpu.SemaphoreType.DMA((pieces,))] * 2
         + [pltpu.SemaphoreType.DMA((batch_axis,))] * 2,
         compiler_params=pltpu.CompilerParams(
-            collective_id=0, has_side_effects=True, vmem_limit_bytes=48 * 1024 * 1024
+            collective_id=0, has_side_effects=True, vmem_limit_bytes=40 * 1024 * 1024
         ),
-    )(first_state[0], guess_points[0, 0], weights.reshape(BLOCK, 3, 3 * channels, channels))
+    )(*(pltpu.with_memory_space_constraint(x, pltpu.HBM) for x in (first_state[0], guess_points[0, 0], weights.reshape(BLOCK, 3, 3 * channels, channels))))
     return (states[:, None], norms[0, :1])
 
 

time: 136 us -> 108 us (0.79)
  Pallas kernels: 127 us -> 105 us
  local copies, waits for them, and re-layouts: 7.74 us -> 2.53 us
    pallas_call x1, Pallas kernels: 127 us -> 105 us  [per_device_streamed(): pl.pallas_call(functools.partial(cycle_kernel, layers_axis, batch_axis),...]
    unnamed x5 -> x1, local copies, waits for them, and re-layouts: 7.23 us -> 2.01 us
where the time goes in v1:
time: 108 us
  Pallas kernels  105 us (97%)
  local copies, waits for them, and re-layouts  2.53 us (2%)
    pallas_call x1, Pallas kernels, per_device_streamed(): pl.pallas_call(functools.partial(cycle_kernel, layers_axis, batch_axis),...  105 us

profile of v1, /device:TPU:26, one launch (start us, length us, event | category | flops | bytes accessed | tf_op | source)
XLA Modules:
  0.0 107.7 jit_solution(7965585127638080823)
XLA Ops:
  0.6 104.5 %shard_map.50 = (f32[4,32,32,256]{3,2,1,0:T(8,128)S(1)}, f32[8,128]{1,0:T(8,128)S(1)}) custom-call(f32[32,32,256]{2,1,0:T(8,128)} %bitcast.9, f32[32,32,256]{2,1,0:T(8,128)} %bitcast.10, bf16[4,3,768,256]{3,2,1,0:T(8,128)(2,1)} %bitcast.8), custom_call_target="tpu_custom_call" | custom-call | tf_op jit(solution)/shard_map/pallas_call | solution.py:460
  105.2 0.5 slice.3
  105.7 2.0 %copy.7 = f32[4,1,32,32,256]{4,3,2,1,0:T(8,128)} copy(f32[4,1,32,32,256]{4,3,2,1,0:T(8,128)S(1)} %bitcast.7) | data formatting | bytes 8388608

commit v2 on v1

--- a/solution.py
+++ b/solution.py
@@ -421,8 +421,9 @@
 
         @pl.when(me == last)
         def _():
-            lax.fori_loop(pieces - 2, pieces, second_body, 0)
-            lax.fori_loop(pieces - 3, pieces, third_body, 0)
+            run(taps_1, 1, PASS_ROWS, sweep_middle(1, PASS_ROWS, taps_2))(passes - 1, 0)
+            third_body(pieces - 3, 0)
+            run(taps_2, 2, PASS_ROWS, sweep_middle(2, PASS_ROWS, None))(passes - 1, 0)
 
         @pl.when(me < last)
         def _():

time: 108 us -> 107 us (level)
  no operation moved by 1% of the time
where the time goes in v2:
time: 107 us
  Pallas kernels  104 us (97%)
  local copies, waits for them, and re-layouts  2.53 us (2%)
    pallas_call x1, Pallas kernels, per_device_streamed(): pl.pallas_call(functools.partial(cycle_kernel, layers_axis, batch_axis),...  104 us

profile of v2, /device:TPU:26, one launch (start us, length us, event | category | flops | bytes accessed | tf_op | source)
XLA Modules:
  0.0 106.8 jit_solution(7505657726067158658)
XLA Ops:
  0.6 103.6 %shard_map.50 = (f32[4,32,32,256]{3,2,1,0:T(8,128)S(1)}, f32[8,128]{1,0:T(8,128)S(1)}) custom-call(f32[32,32,256]{2,1,0:T(8,128)} %bitcast.9, f32[32,32,256]{2,1,0:T(8,128)} %bitcast.10, bf16[4,3,768,256]{3,2,1,0:T(8,128)(2,1)} %bitcast.8), custom_call_target="tpu_custom_call" | custom-call | tf_op jit(solution)/shard_map/pallas_call | solution.py:461
  104.3 0.5 slice.3
  104.8 2.0 %copy.7 = f32[4,1,32,32,256]{4,3,2,1,0:T(8,128)} copy(f32[4,1,32,32,256]{4,3,2,1,0:T(8,128)S(1)} %bitcast.7) | data formatting | bytes 8388608
